TPU v7x, 32 devices: a whole 2x2x4 slice. The times are simulated.
32 devices in a mesh: grp: 8 (over y, x, core), seq: 4 (over z).
Axes of the slice: x: 2, y: 2, z: 4, core: 2. Of those that a mesh axis runs over, the one named last changes fastest.
Arguments:
- inputs: bfloat16 [8, 2, 1536, 768], P('grp', None, 'seq'), may hold values from -6 to 6
- clip_frames: int32 [8, 2], P('grp'), may hold values from 96 to 384, as said below
- cotangent: bfloat16 [8, 2, 1536, 768], P('grp', None, 'seq'), may hold values from -6 to 6
- w_query: bfloat16 [768, 768], P(('grp', 'seq')), may hold values from -0.3125 to 0.3125
- w_key: bfloat16 [768, 768], P(('grp', 'seq')), may hold values from -0.3125 to 0.3125
- w_value: bfloat16 [768, 768], P(('grp', 'seq')), may hold values from -0.21875 to 0.21875
- w_out: bfloat16 [768, 768], P(('grp', 'seq')), may hold values from -0.875 to 0.875
- w_up: bfloat16 [768, 3072], P(('grp', 'seq')), may hold values from -0.21875 to 0.21875
- w_down: bfloat16 [3072, 768], P(('grp', 'seq')), may hold values from -0.15625 to 0.15625
- b_query: bfloat16 [768], P(('grp', 'seq')), may hold values from -3 to 3
- b_value: bfloat16 [768], P(('grp', 'seq')), may hold values from -1.796875 to 1.796875
- b_out: bfloat16 [768], P(('grp', 'seq')), may hold values from -3 to 3
- b_up: bfloat16 [3072], P(('grp', 'seq')), may hold values from -3 to 3
- b_down: bfloat16 [768], P(('grp', 'seq')), may hold values from -3 to 3
- gain_one: bfloat16 [768], P(('grp', 'seq')), may hold values from 0.5 to 1.5
- shift_one: bfloat16 [768], P(('grp', 'seq')), may hold values from -1.796875 to 1.796875
- gain_two: bfloat16 [768], P(('grp', 'seq')), may hold values from 0.5 to 1.5
- shift_two: bfloat16 [768], P(('grp', 'seq')), may hold values from -1.796875 to 1.796875
Outputs:
- layer_out: bfloat16 [8, 2, 1536, 768], P('grp', None, 'seq')
- grad_inputs: bfloat16 [8, 2, 1536, 768], P('grp', None, 'seq')
- grad_w_query: float32 [768, 768], P(('grp', 'seq'))
- grad_w_key: float32 [768, 768], P(('grp', 'seq'))
- grad_w_value: float32 [768, 768], P(('grp', 'seq'))
- grad_w_out: float32 [768, 768], P(('grp', 'seq'))
- grad_w_up: float32 [768, 3072], P(('grp', 'seq'))
- grad_w_down: float32 [3072, 768], P(('grp', 'seq'))
- grad_b_query: float32 [768], P(('grp', 'seq'))
- grad_b_value: float32 [768], P(('grp', 'seq'))
- grad_b_out: float32 [768], P(('grp', 'seq'))
- grad_b_up: float32 [3072], P(('grp', 'seq'))
- grad_b_down: float32 [768], P(('grp', 'seq'))
- grad_gain_one: float32 [768], P(('grp', 'seq'))
- grad_shift_one: float32 [768], P(('grp', 'seq'))
- grad_gain_two: float32 [768], P(('grp', 'seq'))
- grad_shift_two: float32 [768], P(('grp', 'seq'))
Inputs may be any that keep to these rules, and one draw needn't show every extreme that they name: Every slice of clip slot (g, s) holds clip_frames[g, s] live frames at its start; in every draw one slot has exactly 384 and another exactly 96.
All inputs are finite; a program needn't handle non-finite values.
Results may differ from a plain program's by a relative error of at most 0.015.
Values may be sent and summed in bfloat16 or wider, within the bound.
A program may use at most 192 MiB of HBM per device.

v0:
```python
import jax
import jax.numpy as jnp
from jax import lax
from jax.sharding import PartitionSpec as P

HEAD = 64
epsilon = 1e-05
score_scale = 0.125
sqrt_half = 0.7071067811865476
inv_root_tau = 0.3989422804014327


def standardize(token_rows):
    row_mean = jnp.mean(token_rows, -1, keepdims=True)
    centred = token_rows - row_mean
    inverse = lax.rsqrt(jnp.mean(centred * centred, -1, keepdims=True) + epsilon)
    return (centred * inverse, inverse)


def norm_back(grad_out, normed, inverse, gain_vec):
    scaled = grad_out * gain_vec
    grad_rows = inverse * (
        scaled
        - jnp.mean(scaled, -1, keepdims=True)
        - normed * jnp.mean(scaled * normed, -1, keepdims=True)
    )
    return (grad_rows, jnp.sum(grad_out * normed, 0), jnp.sum(grad_out, 0))


def gelu_slope(hidden):
    return (
        0.5 * (1.0 + lax.erf(hidden * sqrt_half))
        + hidden * jnp.exp(-0.5 * hidden * hidden) * inv_root_tau
    )


def split_heads(block, pair_count):
    slot_count, length, width = block.shape
    return block.reshape(slot_count, length, pair_count, 2, HEAD).transpose(2, 0, 1, 3, 4)


def merge_heads(block):
    pair_count, slot_count, length, twin_heads, head_size = block.shape
    return block.transpose(1, 2, 0, 3, 4).reshape(
        slot_count, length, pair_count * twin_heads * head_size
    )


def body(
    inputs,
    clip_frames,
    cotangent,
    w_query,
    w_key,
    w_value,
    w_out,
    w_up,
    w_down,
    b_query,
    b_value,
    b_out,
    b_up,
    b_down,
    gain_one,
    shift_one,
    gain_two,
    shift_two,
):
    shards = (
        w_query,
        w_key,
        w_value,
        w_out,
        w_up,
        w_down,
        b_query,
        b_value,
        b_out,
        b_up,
        b_down,
        gain_one,
        shift_one,
        gain_two,
        shift_two,
    )
    (
        wq_full,
        wk_full,
        wv_full,
        wo_full,
        up_full,
        down_full,
        bq_full,
        bv_full,
        bo_full,
        bu_full,
        bd_full,
        gain_first,
        shift_first,
        gain_second,
        shift_second,
    ) = (
        lax.all_gather(shards[0], ("grp", "seq"), axis=0, tiled=True),
        lax.all_gather(shards[1], ("grp", "seq"), axis=0, tiled=True),
        lax.all_gather(shards[2], ("grp", "seq"), axis=0, tiled=True),
        lax.all_gather(shards[3], ("grp", "seq"), axis=0, tiled=True),
        lax.all_gather(shards[4], ("grp", "seq"), axis=0, tiled=True),
        lax.all_gather(shards[5], ("grp", "seq"), axis=0, tiled=True),
        lax.all_gather(shards[6], ("grp", "seq"), axis=0, tiled=True),
        lax.all_gather(shards[7], ("grp", "seq"), axis=0, tiled=True),
        lax.all_gather(shards[8], ("grp", "seq"), axis=0, tiled=True),
        lax.all_gather(shards[9], ("grp", "seq"), axis=0, tiled=True),
        lax.all_gather(shards[10], ("grp", "seq"), axis=0, tiled=True),
        lax.all_gather(shards[11], ("grp", "seq"), axis=0, tiled=True),
        lax.all_gather(shards[12], ("grp", "seq"), axis=0, tiled=True),
        lax.all_gather(shards[13], ("grp", "seq"), axis=0, tiled=True),
        lax.all_gather(shards[14], ("grp", "seq"), axis=0, tiled=True),
    )
    slot_count, slice_len, width = (inputs.shape[1], inputs.shape[2], inputs.shape[3])
    row_count = slot_count * slice_len
    pair_count = width // (2 * HEAD)
    token_rows = inputs[0].astype(jnp.float32).reshape(row_count, width)
    normed_one, inverse_one = standardize(token_rows)
    first_in = (
        normed_one * gain_first.astype(jnp.float32) + shift_first.astype(jnp.float32)
    ).astype(jnp.bfloat16)
    queries = (
        jnp.dot(first_in, wq_full, preferred_element_type=jnp.float32) + bq_full.astype(jnp.float32)
    ).astype(jnp.bfloat16)
    key_local = jnp.dot(first_in, wk_full, preferred_element_type=jnp.float32).astype(jnp.bfloat16)
    value_local = (
        jnp.dot(first_in, wv_full, preferred_element_type=jnp.float32) + bv_full.astype(jnp.float32)
    ).astype(jnp.bfloat16)
    key_all, value_all = (
        lax.all_gather(key_local.reshape(slot_count, slice_len, width), "seq", axis=1, tiled=True),
        lax.all_gather(
            value_local.reshape(slot_count, slice_len, width), "seq", axis=1, tiled=True
        ),
    )
    clip_len = key_all.shape[1]
    offsets = jnp.arange(clip_len, dtype=jnp.int32) % slice_len
    live_keys = offsets[None, :] < clip_frames[0][:, None]
    query_heads = split_heads(queries.reshape(slot_count, slice_len, width), pair_count)
    key_heads = split_heads(key_all, pair_count)
    value_heads = split_heads(value_all, pair_count)

    def masked_scores(query_block, key_block, live_mask):
        scores = (
            jnp.einsum(
                "cqhd,ckhd->chqk", query_block, key_block, preferred_element_type=jnp.float32
            )
            * score_scale
        )
        return jnp.where(live_mask[:, None, None, :], scores, -1e30)

    def attend(pieces):
        query_block, key_block, value_block = pieces
        scores = masked_scores(query_block, key_block, live_keys)
        row_max = jnp.max(scores, -1, keepdims=True)
        exponent = jnp.exp(scores - row_max)
        row_sum = jnp.sum(exponent, -1, keepdims=True)
        weights = (exponent / row_sum).astype(jnp.bfloat16)
        mixed_block = jnp.einsum(
            "chqk,ckhd->cqhd", weights, value_block, preferred_element_type=jnp.float32
        )
        return (mixed_block, (row_max + jnp.log(row_sum))[..., 0])

    mixed_heads, logsum = lax.map(attend, (query_heads, key_heads, value_heads))
    mixed_low = merge_heads(mixed_heads).reshape(row_count, width).astype(jnp.bfloat16)
    branch = jnp.dot(mixed_low, wo_full, preferred_element_type=jnp.float32) + bo_full.astype(
        jnp.float32
    )
    middle = token_rows + branch
    normed_two, inverse_two = standardize(middle)
    second_in = (
        normed_two * gain_second.astype(jnp.float32) + shift_second.astype(jnp.float32)
    ).astype(jnp.bfloat16)
    hidden = jnp.dot(second_in, up_full, preferred_element_type=jnp.float32) + bu_full.astype(
        jnp.float32
    )
    active_low = jax.nn.gelu(hidden, approximate=False).astype(jnp.bfloat16)
    result = (
        middle
        + jnp.dot(active_low, down_full, preferred_element_type=jnp.float32)
        + bd_full.astype(jnp.float32)
    )
    layer_out = result.astype(jnp.bfloat16).reshape(inputs.shape)
    (
        wq_full,
        wk_full,
        wv_full,
        wo_full,
        up_full,
        down_full,
        bq_full,
        bv_full,
        bo_full,
        bu_full,
        bd_full,
        gain_first,
        shift_first,
        gain_second,
        shift_second,
    ) = (
        lax.all_gather(shards[0], ("grp", "seq"), axis=0, tiled=True),
        lax.all_gather(shards[1], ("grp", "seq"), axis=0, tiled=True),
        lax.all_gather(shards[2], ("grp", "seq"), axis=0, tiled=True),
        lax.all_gather(shards[3], ("grp", "seq"), axis=0, tiled=True),
        lax.all_gather(shards[4], ("grp", "seq"), axis=0, tiled=True),
        lax.all_gather(shards[5], ("grp", "seq"), axis=0, tiled=True),
        lax.all_gather(shards[6], ("grp", "seq"), axis=0, tiled=True),
        lax.all_gather(shards[7], ("grp", "seq"), axis=0, tiled=True),
        lax.all_gather(shards[8], ("grp", "seq"), axis=0, tiled=True),
        lax.all_gather(shards[9], ("grp", "seq"), axis=0, tiled=True),
        lax.all_gather(shards[10], ("grp", "seq"), axis=0, tiled=True),
        lax.all_gather(shards[11], ("grp", "seq"), axis=0, tiled=True),
        lax.all_gather(shards[12], ("grp", "seq"), axis=0, tiled=True),
        lax.all_gather(shards[13], ("grp", "seq"), axis=0, tiled=True),
        lax.all_gather(shards[14], ("grp", "seq"), axis=0, tiled=True),
    )
    grad_top = cotangent[0].reshape(row_count, width)
    grad_rows = grad_top.astype(jnp.float32)
    grad_down = jnp.dot(active_low.T, grad_top, preferred_element_type=jnp.float32)
    gbias_down = jnp.sum(grad_rows, 0)
    grad_active = jnp.dot(grad_top, down_full.T, preferred_element_type=jnp.float32)
    grad_hidden = (grad_active * gelu_slope(hidden)).astype(jnp.bfloat16)
    grad_up = jnp.dot(second_in.T, grad_hidden, preferred_element_type=jnp.float32)
    gbias_up = jnp.sum(grad_hidden.astype(jnp.float32), 0)
    grad_second = jnp.dot(grad_hidden, up_full.T, preferred_element_type=jnp.float32)
    grad_norm_two, grad_gain_two, grad_shift_two = norm_back(
        grad_second, normed_two, inverse_two, gain_second.astype(jnp.float32)
    )
    grad_middle = grad_rows + grad_norm_two
    grad_branch = grad_middle.astype(jnp.bfloat16)
    grad_out = jnp.dot(mixed_low.T, grad_branch, preferred_element_type=jnp.float32)
    gbias_out = jnp.sum(grad_branch.astype(jnp.float32), 0)
    grad_mixed = jnp.dot(grad_branch, wo_full.T, preferred_element_type=jnp.float32).astype(
        jnp.bfloat16
    )
    mixed_grad_heads = split_heads(grad_mixed.reshape(slot_count, slice_len, width), pair_count)

    def score_grads(query_block, key_block, value_block, grad_block, logsum_block, live_mask):
        scores = masked_scores(query_block, key_block, live_mask)
        weights = jnp.exp(scores - logsum_block[..., None])
        grad_weights = jnp.einsum(
            "cqhd,ckhd->chqk", grad_block, value_block, preferred_element_type=jnp.float32
        )
        return (weights, grad_weights)

    def attend_back(pieces):
        query_block, key_block, value_block, grad_block, logsum_block = pieces
        weights, grad_weights = score_grads(
            query_block, key_block, value_block, grad_block, logsum_block, live_keys
        )
        inner_sum = jnp.sum(weights * grad_weights, -1, keepdims=True)
        grad_scores = (weights * (grad_weights - inner_sum)).astype(jnp.bfloat16)
        grad_query_block = (
            jnp.einsum(
                "chqk,ckhd->cqhd", grad_scores, key_block, preferred_element_type=jnp.float32
            )
            * score_scale
        )
        grad_key_block = (
            jnp.einsum(
                "chqk,cqhd->ckhd", grad_scores, query_block, preferred_element_type=jnp.float32
            )
            * score_scale
        )
        grad_value_block = jnp.einsum(
            "chqk,cqhd->ckhd",
            weights.astype(jnp.bfloat16),
            grad_block,
            preferred_element_type=jnp.float32,
        )
        return (grad_query_block, grad_key_block, grad_value_block)

    gq_heads, gk_heads, gv_heads = lax.map(
        attend_back, (query_heads, key_heads, value_heads, mixed_grad_heads, logsum)
    )
    key_grads, value_grads = (
        lax.psum_scatter(
            merge_heads(gk_heads).astype(jnp.bfloat16), "seq", scatter_dimension=1, tiled=True
        ).astype(jnp.float32),
        lax.psum_scatter(
            merge_heads(gv_heads).astype(jnp.bfloat16), "seq", scatter_dimension=1, tiled=True
        ).astype(jnp.float32),
    )
    grad_key = key_grads.reshape(row_count, width).astype(jnp.bfloat16)
    grad_value = value_grads.reshape(row_count, width).astype(jnp.bfloat16)
    grad_query = merge_heads(gq_heads).reshape(row_count, width).astype(jnp.bfloat16)
    gw_query = jnp.dot(first_in.T, grad_query, preferred_element_type=jnp.float32)
    gw_key = jnp.dot(first_in.T, grad_key, preferred_element_type=jnp.float32)
    gw_value = jnp.dot(first_in.T, grad_value, preferred_element_type=jnp.float32)
    gbias_query = jnp.sum(grad_query.astype(jnp.float32), 0)
    gbias_value = jnp.sum(grad_value.astype(jnp.float32), 0)
    grad_first = jnp.dot(grad_query, wq_full.T, preferred_element_type=jnp.float32)
    grad_first = grad_first + jnp.dot(grad_key, wk_full.T, preferred_element_type=jnp.float32)
    grad_first = grad_first + jnp.dot(grad_value, wv_full.T, preferred_element_type=jnp.float32)
    grad_norm_one, grad_gain_one, grad_shift_one = norm_back(
        grad_first, normed_one, inverse_one, gain_first.astype(jnp.float32)
    )
    grad_inputs = (grad_middle + grad_norm_one).astype(jnp.bfloat16).reshape(inputs.shape)
    summed_all = (
        lax.psum_scatter(gw_query, ("grp", "seq"), scatter_dimension=0, tiled=True),
        lax.psum_scatter(gw_key, ("grp", "seq"), scatter_dimension=0, tiled=True),
        lax.psum_scatter(gw_value, ("grp", "seq"), scatter_dimension=0, tiled=True),
        lax.psum_scatter(grad_out, ("grp", "seq"), scatter_dimension=0, tiled=True),
        lax.psum_scatter(grad_up, ("grp", "seq"), scatter_dimension=0, tiled=True),
        lax.psum_scatter(grad_down, ("grp", "seq"), scatter_dimension=0, tiled=True),
        lax.psum_scatter(gbias_query, ("grp", "seq"), scatter_dimension=0, tiled=True),
        lax.psum_scatter(gbias_value, ("grp", "seq"), scatter_dimension=0, tiled=True),
        lax.psum_scatter(gbias_out, ("grp", "seq"), scatter_dimension=0, tiled=True),
        lax.psum_scatter(gbias_up, ("grp", "seq"), scatter_dimension=0, tiled=True),
        lax.psum_scatter(gbias_down, ("grp", "seq"), scatter_dimension=0, tiled=True),
        lax.psum_scatter(grad_gain_one, ("grp", "seq"), scatter_dimension=0, tiled=True),
        lax.psum_scatter(grad_shift_one, ("grp", "seq"), scatter_dimension=0, tiled=True),
        lax.psum_scatter(grad_gain_two, ("grp", "seq"), scatter_dimension=0, tiled=True),
        lax.psum_scatter(grad_shift_two, ("grp", "seq"), scatter_dimension=0, tiled=True),
    )
    return (
        layer_out,
        grad_inputs,
        summed_all[0],
        summed_all[1],
        summed_all[2],
        summed_all[3],
        summed_all[4],
        summed_all[5],
        summed_all[6],
        summed_all[7],
        summed_all[8],
        summed_all[9],
        summed_all[10],
        summed_all[11],
        summed_all[12],
        summed_all[13],
        summed_all[14],
    )


def solution(mesh):
    return jax.shard_map(
        body,
        mesh=mesh,
        in_specs=(
            P("grp", None, "seq", None),
            P("grp", None),
            P("grp", None, "seq", None),
            P(("grp", "seq"), None),
            P(("grp", "seq"), None),
            P(("grp", "seq"), None),
            P(("grp", "seq"), None),
            P(("grp", "seq"), None),
            P(("grp", "seq"), None),
            P(("grp", "seq")),
            P(("grp", "seq")),
            P(("grp", "seq")),
            P(("grp", "seq")),
            P(("grp", "seq")),
            P(("grp", "seq")),
            P(("grp", "seq")),
            P(("grp", "seq")),
            P(("grp", "seq")),
        ),
        out_specs=(
            P("grp", None, "seq", None),
            P("grp", None, "seq", None),
            P(("grp", "seq"), None),
            P(("grp", "seq"), None),
            P(("grp", "seq"), None),
            P(("grp", "seq"), None),
            P(("grp", "seq"), None),
            P(("grp", "seq"), None),
            P(("grp", "seq")),
            P(("grp", "seq")),
            P(("grp", "seq")),
            P(("grp", "seq")),
            P(("grp", "seq")),
            P(("grp", "seq")),
            P(("grp", "seq")),
            P(("grp", "seq")),
            P(("grp", "seq")),
        ),
        check_vma=False,
    )
```

profile of v0, /device:TPU:0, one launch (start us, length us, event | category | flops | bytes accessed | tf_op | source)
XLA Modules:
  0.0 1670.7 jit_solution(11885890830249403467)
XLA Ops:
  17.0 42.7 %all-reduce.19 = (bf16[768]{0:T(1024)(128)(2,1)S(1)}, bf16[768]{0:T(1024)(128)(2,1)S(1)}, bf16[768]{0:T(1024)(128)(2,1)S(1)}, bf16[768]{0:T(1024)(128)(2,1)}, bf...) all-reduce(bf16[768]{0:T(1024)(128)(2,1)S(1)} %dynamic-update-slice, ...), channel_id=1, replica_groups=mesh['grp'=8,'seq'=4] {'grp','seq'}, use_global_device_ids=true, to_apply=%add.1 | all-reduce | flops 9216 | bytes 36864
  71.9 51.8 %all-gather.15.cloned.1.call-done = bf16[768,768]{1,0:T(8,128)(2,1)} async-done(((bf16[24,768]{1,0:T(8,128)(2,1)}), bf16[768,768]{1,0:T(8,128)(2,1)}) %all-gather.15.cloned.1.call-update) | async-done | bytes 1179664 | tf_op jit(solution)/shard_map/all_gather | solution.py:104
  135.0 44.6 %all-gather.13.cloned.1.call-done = bf16[768,768]{1,0:T(8,128)(2,1)} async-done(((bf16[24,768]{1,0:T(8,128)(2,1)}), bf16[768,768]{1,0:T(8,128)(2,1)}) %all-gather.13.cloned.1.call-update) | async-done | bytes 1179664 | tf_op jit(solution)/shard_map/all_gather | solution.py:103
  183.1 86.8 %all-gather.11.cloned.1.call-done = bf16[2,1536,768]{1,2,0:T(8,128)(2,1)} async-done(((bf16[2,384,768]{1,2,0:T(8,128)(2,1)}), bf16[2,1536,768]{1,2,0:T(8,128)(2,1)}) %all-gather.11.cloned.1.call-update) | async-done | bytes 4718608 | tf_op jit(solution)/shard_map/all_gather | solution.py:136
  275.0 84.9 %all-gather.17.cloned.1.call-done = bf16[2,1536,768]{1,2,0:T(8,128)(2,1)} async-done(((bf16[2,384,768]{1,2,0:T(8,128)(2,1)}), bf16[2,1536,768]{1,2,0:T(8,128)(2,1)}) %all-gather.17.cloned.1.call-update) | async-done | bytes 4718608 | tf_op jit(solution)/shard_map/all_gather | solution.py:135
  365.0 54.2 %while.28 = (s32[]{:T(128)}, bf16[6,2,384,2,64]{2,4,3,1,0:T(8,128)(2,1)S(1)}, f32[6,2,2,384]{3,2,1,0:T(2,128)}, bf16[6,2,1536,2,64]{2,4,3,1,0:T(8,128)(2,1)}, bf...) while((s32[]{:T(128)}, ...), condition=%wide.region_5.6_spmd.clone, body=%wide.region_2.5_spmd.clone.sunk | while | flops 632292864 | bytes 30550128 | solution.py:168
  425.6 54.9 %all-gather.21.cloned.1.call-done = bf16[768,3072]{1,0:T(8,128)(2,1)} async-done(((bf16[24,3072]{1,0:T(8,128)(2,1)}), bf16[768,3072]{1,0:T(8,128)(2,1)}) %all-gather.21.cloned.1.call-update) | async-done | bytes 4718608 | tf_op jit(solution)/shard_map/all_gather | solution.py:107
  480.5 28.1 %fusion.49 = (bf16[768,3072]{1,0:T(8,128)(2,1)}, f32[768,3072]{1,0:T(8,128)}) fusion(f32[3072]{0:T(1024)} %convert_element_type.182, bf16[768,3072]{1,0:T(8,128)(2,1)} %all-gather.21.cloned.1.call-done, f32[768,768]{1,0:T(8,128)S(1)} %get-tuple-element.288, f32[768]{0:T(1024)} %convert_element_type.180, f32[768]{0:T(1024)S(1)} %convert_element_type.179, ...), kind=kOutput, calls=%fused_computation.59 | convolution fusion | flops 3782541312 | bytes 21258240 | tf_op jit(solution)/shard_map/dot_general | solution.py:178
  508.6 37.1 %all-gather.23.cloned.1.call-done = bf16[3072,768]{1,0:T(8,128)(2,1)} async-done(((bf16[96,768]{1,0:T(8,128)(2,1)}), bf16[3072,768]{1,0:T(8,128)(2,1)}) %all-gather.23.cloned.1.call-update) | async-done | bytes 4718608 | tf_op jit(solution)/shard_map/all_gather | solution.py:108
  545.7 10.2 convert_reduce_fusion
  570.1 201.9 %while.29 = (s32[]{:T(128)}, bf16[6,2,384,2,64]{2,4,3,1,0:T(8,128)(2,1)}, bf16[6,2,1536,2,64]{2,4,3,0,1:T(8,128)(2,1)}, bf16[6,2,1536,2,64]{2,4,3,0,1:T(8,128)(2...) while((s32[]{:T(128)}, ...), condition=%wide.region_12.13_spmd.clone, body=%wide.region_10.12_spmd.clone.sunk | while | flops 1531676160 | bytes 153400592 | solution.py:277
  574.5 8.7 multiply_reduce_fusion.7
  583.2 9.4 multiply_convert_fusion.2
  608.2 8.7 multiply_reduce_fusion.7
  616.9 9.4 multiply_convert_fusion.2
  650.5 9.4 multiply_convert_fusion.2
  684.2 9.4 multiply_convert_fusion.2
  717.8 9.4 multiply_convert_fusion.2
  751.4 9.4 multiply_convert_fusion.2
  771.9 12.5 copy.86
  790.0 12.6 copy.88
  820.3 53.9 %reduce-scatter.25.cloned.1.call-done = bf16[384,1536]{1,0:T(8,128)(2,1)} async-done(((bf16[1536,1536]{1,0:T(8,128)(2,1)}), bf16[384,1536]{1,0:T(8,128)(2,1)}) %reduce-scatter.25.cloned.1.call-update) | async-done | bytes 1179664
  882.9 79.2 %reduce-scatter.27.cloned.1.call-done = bf16[384,1536]{1,0:T(8,128)(2,1)} async-done(((bf16[1536,1536]{1,0:T(8,128)(2,1)}), bf16[384,1536]{1,0:T(8,128)(2,1)}) %reduce-scatter.27.cloned.1.call-update) | async-done | bytes 1179664
  971.6 9.0 fusion.88
  980.9 10.3 fusion.96
  1000.5 8.7 add_convert_fusion
  1020.2 42.8 %all-reduce.18 = (f32[768]{0:T(1024)}, f32[768]{0:T(1024)}, f32[768]{0:T(1024)}, f32[3072]{0:T(1024)}, f32[768]{0:T(1024)}, /*index=5*/f32[768]{0:T(1024)}, f32[768]{0:T(1024)}, f32[768]{0:T(1024)}, f32[768]{0:T(1024)}) all-reduce(f32[768]{0:T(1024)} %reduce_sum.182, ...), channel_id=10, replica_groups=mesh['grp'=8,'seq'=4] {'grp','seq'}, use_global_device_ids=true, to_apply=%region_24.25.clone | all-reduce | flops 9216 | bytes 73728
  1078.8 93.4 %reduce-scatter.19.cloned.1.call-done = f32[24,768]{1,0:T(8,128)} async-done(((f32[768,768]{1,0:T(8,128)}), f32[24,768]{1,0:T(8,128)}) %reduce-scatter.19.cloned.1.call-update) | async-done | bytes 73744 | tf_op jit(solution)/shard_map/reduce_scatter | solution.py:307
  1172.2 103.9 %reduce-scatter.15.cloned.1.call-done = f32[24,768]{1,0:T(8,128)} async-done(((f32[768,768]{1,0:T(8,128)}), f32[24,768]{1,0:T(8,128)}) %reduce-scatter.15.cloned.1.call-update) | async-done | bytes 73744 | tf_op jit(solution)/shard_map/reduce_scatter | solution.py:305
  1276.1 104.6 %reduce-scatter.17.cloned.1.call-done = f32[24,768]{1,0:T(8,128)} async-done(((f32[768,768]{1,0:T(8,128)}), f32[24,768]{1,0:T(8,128)}) %reduce-scatter.17.cloned.1.call-update) | async-done | bytes 73744 | tf_op jit(solution)/shard_map/reduce_scatter | solution.py:306
  1380.8 140.9 %reduce-scatter.21.cloned.1.call-done = f32[24,3072]{1,0:T(8,128)} async-done(((f32[768,3072]{1,0:T(8,128)}), f32[24,3072]{1,0:T(8,128)}) %reduce-scatter.21.cloned.1.call-update) | async-done | bytes 294928 | tf_op jit(solution)/shard_map/reduce_scatter | solution.py:308
  1521.6 142.0 %reduce-scatter.23.cloned.1.call-done = f32[96,768]{1,0:T(8,128)} async-done(((f32[3072,768]{1,0:T(8,128)}), f32[96,768]{1,0:T(8,128)}) %reduce-scatter.23.cloned.1.call-update) | async-done | bytes 294928 | tf_op jit(solution)/shard_map/reduce_scatter | solution.py:309
  (318 shorter events, 327.1 us)
Async XLA Ops:
  7.2 56.4 %copy-start.2 = (bf16[1,2,384,768]{3,2,1,0:T(8,128)(2,1)S(1)}, bf16[1,2,384,768]{3,2,1,0:T(8,128)(2,1)}, u32[]{:S(2)}) copy-start(bf16[1,2,384,768]{3,2,1,0:T(8,128)(2,1)} %param.22) | copy-start | bytes 3538948
  7.2 60.8 %all-gather.9.cloned.1.call-start = ((), (), s32[]{:S(2)}) async-start(), calls=%async_computation.8 | async-start | bytes 1216512 | tf_op jit(solution)/shard_map/all_gather | solution.py:105
  7.9 115.8 %all-gather.15.cloned.1.call-start = ((), (), s32[]{:S(2)}) async-start(), calls=%async_computation.11 | async-start | bytes 1216512 | tf_op jit(solution)/shard_map/all_gather | solution.py:104
  8.7 170.9 %all-gather.13.cloned.1.call-start = ((), (), s32[]{:S(2)}) async-start(), calls=%async_computation.10 | async-start | bytes 1216512 | tf_op jit(solution)/shard_map/all_gather | solution.py:103
  9.4 260.5 %all-gather.11.cloned.1.call-start = ((), (), s32[]{:S(2)}) async-start(), calls=%async_computation.9 | async-start | bytes 5898240 | tf_op jit(solution)/shard_map/all_gather | solution.py:136
  71.8 288.1 %all-gather.17.cloned.1.call-start = ((), (), s32[]{:S(2)}) async-start(), calls=%async_computation.12 | async-start | bytes 5898240 | tf_op jit(solution)/shard_map/all_gather | solution.py:135
  127.5 294.2 %all-gather.19.cloned.1.call-start = ((), (), s32[]{:S(2)}) async-start(), calls=%async_computation.13 | async-start | bytes 1216512 | tf_op jit(solution)/shard_map/all_gather | solution.py:106
  128.1 352.4 %all-gather.21.cloned.1.call-start = ((), (), s32[]{:S(2)}) async-start(), calls=%async_computation.14 | async-start | bytes 4866048 | tf_op jit(solution)/shard_map/all_gather | solution.py:107
  128.8 416.9 %all-gather.23.cloned.1.call-start = ((), (), s32[]{:S(2)}) async-start(), calls=%async_computation.15 | async-start | bytes 4866048 | tf_op jit(solution)/shard_map/all_gather | solution.py:108
  129.6 744.6 %reduce-scatter.25.cloned.1.call-start = ((), (), s32[]{:S(2)}) async-start(), calls=%async_computation.22 | async-start | bytes 5898240
  425.6 120.1 %copy-start.8 = (bf16[1,2,384,768]{3,2,1,0:T(8,128)(2,1)S(1)}, bf16[1,2,384,768]{3,2,1,0:T(8,128)(2,1)}, u32[]{:S(2)}) copy-start(bf16[1,2,384,768]{3,2,1,0:T(8,128)(2,1)} %param.24) | copy-start | bytes 3538948
  545.7 10.2 copy-start.18
  545.7 10.2 copy-start.37
  573.7 9.5 copy-start.1
  592.6 9.2 copy-start
  607.4 9.5 copy-start.1
  626.3 9.2 copy-start
  641.0 9.5 copy-start.1
  674.6 9.5 copy-start.1
  693.5 9.2 copy-start
  708.2 9.5 copy-start.1
  727.1 9.2 copy-start
  741.9 9.5 copy-start.1
  760.8 9.3 copy-start
  789.9 172.2 %reduce-scatter.27.cloned.1.call-start = ((), (), s32[]{:S(2)}) async-start(), calls=%async_computation.23 | async-start | bytes 5898240
  808.0 270.8 %reduce-scatter.13.cloned.1.call-start = ((), (), s32[]{:S(2)}) async-start(), calls=%async_computation.16 | async-start | bytes 2433024 | tf_op jit(solution)/shard_map/reduce_scatter | solution.py:304
  815.6 356.6 %reduce-scatter.19.cloned.1.call-start = ((), (), s32[]{:S(2)}) async-start(), calls=%async_computation.19 | async-start | bytes 2433024 | tf_op jit(solution)/shard_map/reduce_scatter | solution.py:307
  820.2 455.9 %reduce-scatter.15.cloned.1.call-start = ((), (), s32[]{:S(2)}) async-start(), calls=%async_computation.17 | async-start | bytes 2433024 | tf_op jit(solution)/shard_map/reduce_scatter | solution.py:305
  882.9 497.9 %reduce-scatter.17.cloned.1.call-start = ((), (), s32[]{:S(2)}) async-start(), calls=%async_computation.18 | async-start | bytes 2433024 | tf_op jit(solution)/shard_map/reduce_scatter | solution.py:306
  970.9 550.7 %reduce-scatter.21.cloned.1.call-start = ((), (), s32[]{:S(2)}) async-start(), calls=%async_computation.20 | async-start | bytes 9732096 | tf_op jit(solution)/shard_map/reduce_scatter | solution.py:308
  980.6 683.1 %reduce-scatter.23.cloned.1.call-start = ((), (), s32[]{:S(2)}) async-start(), calls=%async_computation.21 | async-start | bytes 9732096 | tf_op jit(solution)/shard_map/reduce_scatter | solution.py:309
  1016.4 59.3 %copy-start.7 = (f32[768,768]{1,0:T(8,128)S(1)}, f32[768,768]{1,0:T(8,128)}, u32[]{:S(2)}) copy-start(f32[768,768]{1,0:T(8,128)} %copy-done.6) | copy-start | bytes 7077892
  (40 other events, 104.8 us)
Sparse Core Ops, SparseCore 0:
  10.8 57.1 all-gather.8
  70.8 52.8 all-gather.14
  126.5 53.0 all-gather.12
  181.6 88.2 all-gather.10
  272.0 87.8 all-gather.16
  362.5 52.6 all-gather.18
  418.0 62.4 all-gather.20
  483.3 62.3 all-gather.22
  790.0 84.0 reduce-scatter.24
  876.3 85.7 reduce-scatter.26
  968.0 99.5 reduce-scatter.12
  1074.1 98.0 reduce-scatter.18
  1178.1 98.0 reduce-scatter.14
  1282.7 98.0 reduce-scatter.16
  1387.1 134.5 reduce-scatter.20
  1529.0 134.6 reduce-scatter.22
where the time goes:
time: 1680 us; the launch traced here: 1670 us
  waiting for transfers between devices  1090 us (65%)
  matrix products  278 us (17%)
  local copies, waits for them, and re-layouts  110 us (7%)
  other arithmetic  95 us (6%)
  blocking collectives  85.5 us (5%)
    reduce_scatter x1, waiting for transfers between devices, body(): lax.psum_scatter(grad_down, ('grp', 'seq'), scatter_dimension=0, tiled=True)  142 us
    reduce_scatter x1, waiting for transfers between devices, body(): lax.psum_scatter(grad_up, ('grp', 'seq'), scatter_dimension=0, tiled=True)  141 us
    unnamed x18, waiting for transfers between devices  137 us
    reduce_scatter x1, waiting for transfers between devices, body(): lax.psum_scatter(gw_value, ('grp', 'seq'), scatter_dimension=0, tiled=True)  105 us
    reduce_scatter x1, waiting for transfers between devices, body(): lax.psum_scatter(gw_key, ('grp', 'seq'), scatter_dimension=0, tiled=True)  104 us
    reduce_scatter x1, waiting for transfers between devices, body(): lax.psum_scatter(grad_out, ('grp', 'seq'), scatter_dimension=0, tiled=True)  93.4 us
    all_gather x1, waiting for transfers between devices, body(): lax.all_gather(value_local.reshape(slot_count, slice_len, width), 'seq',...  86.8 us
    unnamed x2, blocking collectives  85.5 us
  transfers between devices with their start and end apart: 16, of which 14 were waited for; matrix products, arithmetic and copies ran while one was open for 14% of the time, Pallas kernels for 0%

commit v1 on v0

--- a/solution.py
+++ b/solution.py
@@ -8,6 +8,12 @@
 score_scale = 0.125
 sqrt_half = 0.7071067811865476
 inv_root_tau = 0.3989422804014327
+
+
+def plan_positions(payload, axis_no):
+    s_next = list(payload.shape[1:])
+    s_next[axis_no] *= payload.shape[0]
+    return jnp.moveaxis(payload, 0, axis_no).reshape(s_next)
 
 
 def standardize(token_rows):
@@ -131,11 +137,35 @@
     value_local = (
         jnp.dot(first_in, wv_full, preferred_element_type=jnp.float32) + bv_full.astype(jnp.float32)
     ).astype(jnp.bfloat16)
+
+    def _enter_regions(values, mesh_dim, axis_k):
+        world_n = jax.lax.psum(1, axis_name=mesh_dim)
+        pieces_in = tuple(((tick, (tick + 1) % world_n) for tick in range(world_n)))
+        nodes = tuple(((j0, dev_j) for dev_j, j0 in pieces_in))
+        v1, plain = ([], [])
+        hop_no = 0
+        while hop_no < world_n - 1:
+            if hop_no % 2 == 0:
+                h_now = jax.lax.ppermute(
+                    v1[-1] if v1 else values, axis_name=mesh_dim, perm=pieces_in
+                )
+                v1.append(h_now)
+            else:
+                placed = jax.lax.ppermute(
+                    plain[-1] if plain else values, axis_name=mesh_dim, perm=nodes
+                )
+                plain.append(placed)
+            hop_no = hop_no + 1
+        local_out = jnp.stack([*v1[::-1], values, *plain], axis=0)
+        built = jax.lax.axis_index(mesh_dim)
+        newest = len(v1)
+        x_new = built - newest
+        local_out = local_out[(jnp.arange(world_n) - x_new) % world_n]
+        return plan_positions(local_out, axis_k)
+
     key_all, value_all = (
         lax.all_gather(key_local.reshape(slot_count, slice_len, width), "seq", axis=1, tiled=True),
-        lax.all_gather(
-            value_local.reshape(slot_count, slice_len, width), "seq", axis=1, tiled=True
-        ),
+        _enter_regions(value_local.reshape(slot_count, slice_len, width), "seq", 1),
     )
     clip_len = key_all.shape[1]
     offsets = jnp.arange(clip_len, dtype=jnp.int32) % slice_len

time: 1680 us -> 1620 us (0.964)
  waiting for transfers between devices: 1090 us -> 1000 us
  local copies, waits for them, and re-layouts: 110 us -> 132 us
    all_gather x1 -> x0, waiting for transfers between devices: 86.8 us -> none  [body(): lax.all_gather(value_local.reshape(slot_count, slice_len, width), 'seq',...]
    all_gather x1, waiting for transfers between devices: 51.8 us -> 3.83 us  [body(): lax.all_gather(shards[1], ('grp', 'seq'), axis=0, tiled=True)]
    all_gather x1, waiting for transfers between devices: 3.89 us -> 50 us  [body(): lax.all_gather(shards[2], ('grp', 'seq'), axis=0, tiled=True)]
    all_gather x1, waiting for transfers between devices: 84.9 us -> 52.5 us  [body(): lax.all_gather(key_local.reshape(slot_count, slice_len, width), 'seq', ax...]
    ppermute x0 -> x3, waiting for transfers between devices: none -> 27.9 us  [the longest x2 27.9 us: _enter_regions(): jax.lax.ppermute(v1[-1] if v1 else values, axis_name=mesh_dim, perm=piece...]
    unnamed x18 -> x17, waiting for transfers between devices: 137 us -> 136 us
    unnamed x115 -> x119, local copies, waits for them, and re-layouts: 85.1 us -> 85.2 us
  transfers between devices with their start and end apart: 16 -> 18, of which waited for: 14 -> 14; matrix products, arithmetic and copies ran while one was open for 14% -> 16% of each run, Pallas kernels for 0% -> 0%
where the time goes in v1:
time: 1620 us; the launch traced here: 1610 us
  waiting for transfers between devices  1000 us (62%)
  matrix products  279 us (17%)
  local copies, waits for them, and re-layouts  132 us (8%)
  other arithmetic  97.2 us (6%)
  blocking collectives  85.6 us (5%)
    reduce_scatter x1, waiting for transfers between devices, body(): lax.psum_scatter(grad_down, ('grp', 'seq'), scatter_dimension=0, tiled=True)  142 us
    reduce_scatter x1, waiting for transfers between devices, body(): lax.psum_scatter(grad_up, ('grp', 'seq'), scatter_dimension=0, tiled=True)  141 us
    unnamed x17, waiting for transfers between devices  136 us
    reduce_scatter x1, waiting for transfers between devices, body(): lax.psum_scatter(gw_value, ('grp', 'seq'), scatter_dimension=0, tiled=True)  105 us
    reduce_scatter x1, waiting for transfers between devices, body(): lax.psum_scatter(gw_key, ('grp', 'seq'), scatter_dimension=0, tiled=True)  104 us
    reduce_scatter x1, waiting for transfers between devices, body(): lax.psum_scatter(grad_out, ('grp', 'seq'), scatter_dimension=0, tiled=True)  93.5 us
    unnamed x2, blocking collectives  85.6 us
    unnamed x119, local copies, waits for them, and re-layouts  85.2 us
  transfers between devices with their start and end apart: 18, of which 14 were waited for; matrix products, arithmetic and copies ran while one was open for 16% of the time, Pallas kernels for 0%

profile of v1, /device:TPU:0, one launch (start us, length us, event | category | flops | bytes accessed | tf_op | source)
XLA Modules:
  0.0 1614.7 jit_solution(13753669330162857276)
XLA Ops:
  17.0 42.7 %all-reduce.19 = (bf16[768]{0:T(1024)(128)(2,1)S(1)}, bf16[768]{0:T(1024)(128)(2,1)S(1)}, bf16[768]{0:T(1024)(128)(2,1)}, bf16[768]{0:T(1024)(128)(2,1)}, bf16[7...) all-reduce(bf16[768]{0:T(1024)(128)(2,1)S(1)} %dynamic-update-slice, ...), channel_id=1, replica_groups=mesh['grp'=8,'seq'=4] {'grp','seq'}, use_global_device_ids=true, to_apply=%add.1 | all-reduce | flops 9216 | bytes 36864
  73.7 50.0 %all-gather.8.cloned.1.call-done = bf16[768,768]{1,0:T(8,128)(2,1)} async-done(((bf16[24,768]{1,0:T(8,128)(2,1)}), bf16[768,768]{1,0:T(8,128)(2,1)}) %all-gather.8.cloned.1.call-update) | async-done | bytes 1179664 | tf_op jit(solution)/shard_map/all_gather | solution.py:111
  130.9 27.9 %collective-permute-done = bf16[2,384,768]{2,1,0:T(8,128)(2,1)} collective-permute-done((bf16[2,384,768]{2,1,0:T(8,128)(2,1)}, bf16[2,384,768]{2,1,0:T(8,128)(2,1)}, u32[]{:S(2)}, u32[]{:S(2)}) %collective-permute-start) | collective-permute-done | bytes 1179680 | tf_op jit(solution)/shard_map/ppermute | solution.py:149
  161.4 53.9 %all-gather.10.cloned.1.call-done = bf16[768,768]{1,0:T(8,128)(2,1)} async-done(((bf16[24,768]{1,0:T(8,128)(2,1)}), bf16[768,768]{1,0:T(8,128)(2,1)}) %all-gather.10.cloned.1.call-update) | async-done | bytes 1179664 | tf_op jit(solution)/shard_map/all_gather | solution.py:109
  237.6 8.8 reshape_reshape.11
  251.4 52.5 %all-gather.14.cloned.1.call-done = bf16[2,1536,768]{1,2,0:T(8,128)(2,1)} async-done(((bf16[2,384,768]{1,2,0:T(8,128)(2,1)}), bf16[2,1536,768]{1,2,0:T(8,128)(2,1)}) %all-gather.14.cloned.1.call-update) | async-done | bytes 4718608 | tf_op jit(solution)/shard_map/all_gather | solution.py:167
  309.1 54.2 %while.28 = (s32[]{:T(128)}, bf16[6,2,384,2,64]{2,4,3,1,0:T(8,128)(2,1)S(1)}, f32[6,2,2,384]{3,2,1,0:T(2,128)}, bf16[6,2,1536,2,64]{2,4,3,1,0:T(8,128)(2,1)}, bf...) while((s32[]{:T(128)}, ...), condition=%wide.region_5.6_spmd.clone, body=%wide.region_2.5_spmd.clone.sunk | while | flops 632292864 | bytes 30550128 | solution.py:198
  369.7 54.7 %all-gather.18.cloned.1.call-done = bf16[768,3072]{1,0:T(8,128)(2,1)} async-done(((bf16[24,3072]{1,0:T(8,128)(2,1)}), bf16[768,3072]{1,0:T(8,128)(2,1)}) %all-gather.18.cloned.1.call-update) | async-done | bytes 4718608 | tf_op jit(solution)/shard_map/all_gather | solution.py:113
  424.4 28.1 %fusion.49 = (bf16[768,3072]{1,0:T(8,128)(2,1)}, f32[768,3072]{1,0:T(8,128)}) fusion(f32[3072]{0:T(1024)} %convert_element_type.182, bf16[768,3072]{1,0:T(8,128)(2,1)} %all-gather.18.cloned.1.call-done, f32[768,768]{1,0:T(8,128)S(1)} %get-tuple-element.288, f32[768]{0:T(1024)} %convert_element_type.180, f32[768]{0:T(1024)S(1)} %convert_element_type.179, ...), kind=kOutput, calls=%fused_computation.60 | convolution fusion | flops 3782541312 | bytes 21258240 | tf_op jit(solution)/shard_map/dot_general | solution.py:208
  452.5 37.1 %all-gather.20.cloned.1.call-done = bf16[3072,768]{1,0:T(8,128)(2,1)} async-done(((bf16[96,768]{1,0:T(8,128)(2,1)}), bf16[3072,768]{1,0:T(8,128)(2,1)}) %all-gather.20.cloned.1.call-update) | async-done | bytes 4718608 | tf_op jit(solution)/shard_map/all_gather | solution.py:114
  489.6 10.2 convert_reduce_fusion
  514.0 201.9 %while.29 = (s32[]{:T(128)}, bf16[6,2,384,2,64]{2,4,3,1,0:T(8,128)(2,1)}, bf16[6,2,1536,2,64]{2,4,3,0,1:T(8,128)(2,1)}, bf16[6,2,1536,2,64]{2,4,3,0,1:T(8,128)(2...) while((s32[]{:T(128)}, ...), condition=%wide.region_12.13_spmd.clone, body=%wide.region_10.12_spmd.clone.sunk | while | flops 1531676160 | bytes 153400592 | solution.py:307
  527.1 9.4 multiply_convert_fusion.2
  560.8 9.4 multiply_convert_fusion.2
  585.8 8.7 multiply_reduce_fusion.7
  594.5 9.4 multiply_convert_fusion.2
  628.1 9.4 multiply_convert_fusion.2
  661.8 9.4 multiply_convert_fusion.2
  695.4 9.4 multiply_convert_fusion.2
  715.9 12.5 copy.85
  734.0 12.6 copy.87
  764.3 53.9 %reduce-scatter.25.cloned.1.call-done = bf16[384,1536]{1,0:T(8,128)(2,1)} async-done(((bf16[1536,1536]{1,0:T(8,128)(2,1)}), bf16[384,1536]{1,0:T(8,128)(2,1)}) %reduce-scatter.25.cloned.1.call-update) | async-done | bytes 1179664
  826.9 79.3 %reduce-scatter.27.cloned.1.call-done = bf16[384,1536]{1,0:T(8,128)(2,1)} async-done(((bf16[1536,1536]{1,0:T(8,128)(2,1)}), bf16[384,1536]{1,0:T(8,128)(2,1)}) %reduce-scatter.27.cloned.1.call-update) | async-done | bytes 1179664
  915.7 9.0 fusion.90
  925.0 10.3 fusion.98
  944.6 8.7 add_convert_fusion
  964.3 43.0 %all-reduce.18 = (f32[768]{0:T(1024)}, f32[768]{0:T(1024)}, f32[768]{0:T(1024)}, f32[3072]{0:T(1024)}, f32[768]{0:T(1024)}, /*index=5*/f32[768]{0:T(1024)}, f32[768]{0:T(1024)}, f32[768]{0:T(1024)}, f32[768]{0:T(1024)}) all-reduce(f32[768]{0:T(1024)} %reduce_sum.182, ...), channel_id=10, replica_groups=mesh['grp'=8,'seq'=4] {'grp','seq'}, use_global_device_ids=true, to_apply=%region_24.25.clone | all-reduce | flops 9216 | bytes 73728
  1023.0 93.5 %reduce-scatter.19.cloned.1.call-done = f32[24,768]{1,0:T(8,128)} async-done(((f32[768,768]{1,0:T(8,128)}), f32[24,768]{1,0:T(8,128)}) %reduce-scatter.19.cloned.1.call-update) | async-done | bytes 73744 | tf_op jit(solution)/shard_map/reduce_scatter | solution.py:337
  1116.5 103.8 %reduce-scatter.15.cloned.1.call-done = f32[24,768]{1,0:T(8,128)} async-done(((f32[768,768]{1,0:T(8,128)}), f32[24,768]{1,0:T(8,128)}) %reduce-scatter.15.cloned.1.call-update) | async-done | bytes 73744 | tf_op jit(solution)/shard_map/reduce_scatter | solution.py:335
  1220.2 104.8 %reduce-scatter.17.cloned.1.call-done = f32[24,768]{1,0:T(8,128)} async-done(((f32[768,768]{1,0:T(8,128)}), f32[24,768]{1,0:T(8,128)}) %reduce-scatter.17.cloned.1.call-update) | async-done | bytes 73744 | tf_op jit(solution)/shard_map/reduce_scatter | solution.py:336
  1325.0 140.7 %reduce-scatter.21.cloned.1.call-done = f32[24,3072]{1,0:T(8,128)} async-done(((f32[768,3072]{1,0:T(8,128)}), f32[24,3072]{1,0:T(8,128)}) %reduce-scatter.21.cloned.1.call-update) | async-done | bytes 294928 | tf_op jit(solution)/shard_map/reduce_scatter | solution.py:338
  1465.7 142.0 %reduce-scatter.23.cloned.1.call-done = f32[96,768]{1,0:T(8,128)} async-done(((f32[3072,768]{1,0:T(8,128)}), f32[96,768]{1,0:T(8,128)}) %reduce-scatter.23.cloned.1.call-update) | async-done | bytes 294928 | tf_op jit(solution)/shard_map/reduce_scatter | solution.py:339
  (330 shorter events, 354.7 us)
Async XLA Ops:
  7.2 56.4 %copy-start.2 = (bf16[1,2,384,768]{3,2,1,0:T(8,128)(2,1)S(1)}, bf16[1,2,384,768]{3,2,1,0:T(8,128)(2,1)}, u32[]{:S(2)}) copy-start(bf16[1,2,384,768]{3,2,1,0:T(8,128)(2,1)} %param.22) | copy-start | bytes 3538948
  7.2 60.8 %all-gather.12.cloned.1.call-start = ((), (), s32[]{:S(2)}) async-start(), calls=%async_computation.10 | async-start | bytes 1216512 | tf_op jit(solution)/shard_map/all_gather | solution.py:110
  7.9 115.8 %all-gather.8.cloned.1.call-start = ((), (), s32[]{:S(2)}) async-start(), calls=%async_computation.8 | async-start | bytes 1216512 | tf_op jit(solution)/shard_map/all_gather | solution.py:111
  8.7 206.6 %all-gather.10.cloned.1.call-start = ((), (), s32[]{:S(2)}) async-start(), calls=%async_computation.9 | async-start | bytes 1216512 | tf_op jit(solution)/shard_map/all_gather | solution.py:109
  9.4 294.5 %all-gather.14.cloned.1.call-start = ((), (), s32[]{:S(2)}) async-start(), calls=%async_computation.11 | async-start | bytes 5898240 | tf_op jit(solution)/shard_map/all_gather | solution.py:167
  71.8 294.0 %all-gather.16.cloned.1.call-start = ((), (), s32[]{:S(2)}) async-start(), calls=%async_computation.12 | async-start | bytes 1216512 | tf_op jit(solution)/shard_map/all_gather | solution.py:112
  72.4 352.0 %all-gather.18.cloned.1.call-start = ((), (), s32[]{:S(2)}) async-start(), calls=%async_computation.13 | async-start | bytes 4866048 | tf_op jit(solution)/shard_map/all_gather | solution.py:113
  73.0 416.6 %all-gather.20.cloned.1.call-start = ((), (), s32[]{:S(2)}) async-start(), calls=%async_computation.14 | async-start | bytes 4866048 | tf_op jit(solution)/shard_map/all_gather | solution.py:114
  73.7 85.2 %copy-start.38 = (bf16[768]{0:T(1024)(128)(2,1)S(1)}, bf16[768]{0:T(1024)(128)(2,1)}, u32[]{:S(2)}) copy-start(bf16[768]{0:T(1024)(128)(2,1)} %get-tuple-element.276) | copy-start | bytes 4612
  73.7 85.8 %copy-start.37 = (bf16[768]{0:T(1024)(128)(2,1)S(1)}, bf16[768]{0:T(1024)(128)(2,1)}, u32[]{:S(2)}) copy-start(bf16[768]{0:T(1024)(128)(2,1)} %get-tuple-element.275) | copy-start | bytes 4612
  127.1 31.8 %collective-permute-start = (bf16[2,384,768]{2,1,0:T(8,128)(2,1)}, bf16[2,384,768]{2,1,0:T(8,128)(2,1)}, u32[]{:S(2)}, u32[]{:S(2)}) collective-permute-start(bf16[2,384,768]{2,1,0:T(8,128)(2,1)} %bitcast.1), channel_id=1, source_target_pairs={{0,1},{1,2},{2,3},{3,0},{4,5},{5,6},{6,7},{7,4},{8,9},{9,10},{10,1... | collective-permute-start | bytes 3538952 | tf_op jit(solution)/shard_map/ppermute | solution.py:149
  127.6 91.4 %collective-permute-start.2 = (bf16[2,384,768]{2,1,0:T(8,128)(2,1)}, bf16[2,384,768]{2,1,0:T(8,128)(2,1)}, u32[]{:S(2)}, u32[]{:S(2)}) collective-permute-start(bf16[2,384,768]{2,1,0:T(8,128)(2,1)} %bitcast.1), channel_id=1, source_target_pairs={{1,0},{2,1},{3,2},{0,3},{5,4},{6,5},{7,6},{4,7},{9,8},{10,9},{11,1... | collective-permute-start | bytes 3538952 | tf_op jit(solution)/shard_map/ppermute | solution.py:154
  158.8 60.2 %collective-permute-start.1 = (bf16[2,384,768]{2,1,0:T(8,128)(2,1)}, bf16[2,384,768]{2,1,0:T(8,128)(2,1)}, u32[]{:S(2)}, u32[]{:S(2)}) collective-permute-start(bf16[2,384,768]{2,1,0:T(8,128)(2,1)} %collective-permute-done), channel_id=1, source_target_pairs={{0,1},{1,2},{2,3},{3,0},{4,5},{5,6},{6,7},{7,4},{8,9},{9,10},{10,1... | collective-permute-start | bytes 3538952 | tf_op jit(solution)/shard_map/ppermute | solution.py:149
  158.9 659.3 %reduce-scatter.25.cloned.1.call-start = ((), (), s32[]{:S(2)}) async-start(), calls=%async_computation.21 | async-start | bytes 5898240
  369.7 119.9 %copy-start.8 = (bf16[1,2,384,768]{3,2,1,0:T(8,128)(2,1)S(1)}, bf16[1,2,384,768]{3,2,1,0:T(8,128)(2,1)}, u32[]{:S(2)}) copy-start(bf16[1,2,384,768]{3,2,1,0:T(8,128)(2,1)} %param.24) | copy-start | bytes 3538948
  489.6 10.2 copy-start.18
  489.6 10.2 copy-start.39
  517.6 9.5 copy-start.1
  551.3 9.5 copy-start.1
  570.2 9.3 copy-start
  584.9 9.5 copy-start.1
  618.6 9.5 copy-start.1
  652.2 9.5 copy-start.1
  685.9 9.5 copy-start.1
  733.9 172.3 %reduce-scatter.27.cloned.1.call-start = ((), (), s32[]{:S(2)}) async-start(), calls=%async_computation.22 | async-start | bytes 5898240
  752.0 271.0 %reduce-scatter.13.cloned.1.call-start = ((), (), s32[]{:S(2)}) async-start(), calls=%async_computation.15 | async-start | bytes 2433024 | tf_op jit(solution)/shard_map/reduce_scatter | solution.py:334
  759.6 356.9 %reduce-scatter.19.cloned.1.call-start = ((), (), s32[]{:S(2)}) async-start(), calls=%async_computation.18 | async-start | bytes 2433024 | tf_op jit(solution)/shard_map/reduce_scatter | solution.py:337
  764.2 456.0 %reduce-scatter.15.cloned.1.call-start = ((), (), s32[]{:S(2)}) async-start(), calls=%async_computation.16 | async-start | bytes 2433024 | tf_op jit(solution)/shard_map/reduce_scatter | solution.py:335
  826.9 498.1 %reduce-scatter.17.cloned.1.call-start = ((), (), s32[]{:S(2)}) async-start(), calls=%async_computation.17 | async-start | bytes 2433024 | tf_op jit(solution)/shard_map/reduce_scatter | solution.py:336
  915.0 550.6 %reduce-scatter.21.cloned.1.call-start = ((), (), s32[]{:S(2)}) async-start(), calls=%async_computation.19 | async-start | bytes 9732096 | tf_op jit(solution)/shard_map/reduce_scatter | solution.py:338
  924.7 683.0 %reduce-scatter.23.cloned.1.call-start = ((), (), s32[]{:S(2)}) async-start(), calls=%async_computation.20 | async-start | bytes 9732096 | tf_op jit(solution)/shard_map/reduce_scatter | solution.py:339
  960.5 59.4 %copy-start.7 = (f32[768,768]{1,0:T(8,128)S(1)}, f32[768,768]{1,0:T(8,128)}, u32[]{:S(2)}) copy-start(f32[768,768]{1,0:T(8,128)} %copy-done.6) | copy-start | bytes 7077892
  (44 other events, 141.2 us)
Sparse Core Ops, SparseCore 0:
  10.8 57.1 all-gather.11
  70.8 52.8 all-gather.7
  126.5 88.7 all-gather.9
  217.3 86.5 all-gather.13
  306.6 52.6 all-gather.15
  361.9 62.4 all-gather.17
  427.2 62.3 all-gather.19
  734.0 84.0 reduce-scatter.24
  820.4 85.7 reduce-scatter.26
  912.0 99.6 reduce-scatter.12
  1018.4 98.0 reduce-scatter.18
  1122.2 97.9 reduce-scatter.14
  1226.9 98.0 reduce-scatter.16
  1331.3 134.3 reduce-scatter.20
  1473.0 134.6 reduce-scatter.22
